TPU v7x, 256 devices: a whole 4x4x8 slice. The times are simulated.
256 devices in a mesh: factor: 16 (over x_hi, z), col: 16 (over x_lo, y, core).
Axes of the slice: x: 4 (x_hi: 2, x_lo: 2; x = x_hi * 2 + x_lo), y: 4, z: 8, core: 2. Of those that a mesh axis runs over, the one named last changes fastest.
Arguments:
- activations: bfloat16 [16384, 2048], P('factor', 'col'), may hold values from -2.5 to 2.5
- targets: bfloat16 [16384, 2048], P('factor', 'col'), may hold values from -6 to 6
- diagonal: float32 [14, 16384], P(None, 'factor'), may hold values from 0.6 to 0.8
- crossing: float32 [14, 16384], P(None, 'factor'), may hold values from -2.5 to 2.5
Outputs:
- new_diagonal: float32 [14, 16384], P(None, 'factor')
- new_crossing: float32 [14, 16384], P(None, 'factor')
- residual: float32 [16384, 2048], P('factor', 'col')
All inputs are finite; a program needn't handle non-finite values.
Results may differ from a plain program's by a relative error of at most 0.0003.
Values sent between devices are 32-bit elements; how exact they have to be, the bound alone decides.
A program may use at most 64 MiB of HBM per device.

v0:
```python
import jax
import jax.numpy as jnp
import numpy as np
from jax import lax
from jax.sharding import PartitionSpec as P

step_scale = 0.03


def partner(block, axis, distance):
    count = lax.axis_size(axis)
    route = []
    for low in range(count):
        high = low | 1 << distance
        if high != low and high < count:
            route += [(low, high), (high, low)]
    return lax.ppermute(block, axis, route)


def reversal(count):
    bits = count.bit_length() - 1
    places = np.arange(count)
    result = np.zeros(count, dtype=np.int32)
    for place in range(bits):
        result = result | (places >> place & 1) << bits - 1 - place
    return result


def partner_rows(values, stride):
    height = values.shape[0]
    folded = values.reshape((height // (2 * stride), 2, stride) + values.shape[1:])
    return jnp.flip(folded, 1).reshape(values.shape)


def to_owner(values, groups):
    height = values.shape[0]
    shaped = values.reshape((height // groups, groups) + values.shape[1:])
    return shaped[:, reversal(groups)]


def per_device(activations, targets, diagonal, crossing):
    height, width = activations.shape
    sections = diagonal.shape[0]
    groups = lax.axis_size("factor")
    row_bits = height.bit_length() - 1
    total = width * lax.axis_size("col")
    order = reversal(height)
    goal = targets.astype(jnp.float32)
    field_in = activations.astype(jnp.float32)
    saved = []
    diag_terms = [None] * sections
    cross_terms = [None] * sections
    field = field_in
    for level in range(sections):
        if level < row_bits:
            beside = partner_rows(field, 2**level)
        else:
            beside = partner(field, "factor", level - row_bits)
        saved.append((field, beside))
        field = diagonal[level][:, None] * field + crossing[level][:, None] * beside
    moved = lax.all_to_all(
        to_owner(field, groups), "factor", split_axis=1, concat_axis=0, tiled=True
    )
    output = moved.reshape(height, width)[order]
    error = output - goal
    scaled = 2.0 / total * error
    arrived = lax.all_to_all(
        to_owner(scaled, groups), "factor", split_axis=1, concat_axis=0, tiled=True
    )
    gradient = arrived.reshape(height, width)[order]
    for level in range(sections - 1, row_bits - 1, -1):
        field_s, beside = saved[level]
        diag_terms[level] = jnp.sum(gradient * field_s, axis=1)
        cross_terms[level] = jnp.sum(gradient * beside, axis=1)
        carried = crossing[level][:, None] * gradient
        returned = partner(carried, "factor", level - row_bits)
        gradient = diagonal[level][:, None] * gradient + returned
    for level in range(row_bits - 1, -1, -1):
        field_s, beside = saved[level]
        diag_terms[level] = jnp.sum(gradient * field_s, axis=1)
        cross_terms[level] = jnp.sum(gradient * beside, axis=1)
        if level > 0:
            carried = crossing[level][:, None] * gradient
            gradient = diagonal[level][:, None] * gradient + partner_rows(carried, 2**level)
    grad_diag = jnp.stack(diag_terms, axis=0)
    grad_cross = jnp.stack(cross_terms, axis=0)
    grad_diag, grad_cross = lax.psum((grad_diag, grad_cross), "col")
    diagonal = diagonal - step_scale * grad_diag
    crossing = crossing - step_scale * grad_cross
    return (diagonal, crossing, error)


def solution(mesh):
    placed = (P("factor", "col"), P("factor", "col"), P(None, "factor"), P(None, "factor"))
    return jax.shard_map(
        per_device,
        mesh=mesh,
        in_specs=placed,
        out_specs=(P(None, "factor"), P(None, "factor"), P("factor", "col")),
        check_vma=False,
    )
```

profile of v0, /device:TPU:1, one launch (start us, length us, event | category | flops | bytes accessed | tf_op | source)
XLA Modules:
  0.0 423.2 jit_solution(4129885722539323021)
XLA Ops:
  9.6 2.5 rev.67
  20.8 2.2 fusion.4
  23.0 2.0 rev.75
  24.9 2.2 fusion.2
  27.1 1.9 rev.76
  30.5 2.6 collective-permute-start
  33.0 10.6 %collective-permute-done = f32[1024,128]{1,0:T(8,128)S(1)} collective-permute-done((f32[1024,128]{1,0:T(8,128)S(1)}, f32[1024,128]{1,0:T(8,128)S(1)}, u32[]{:S(2)}, u32[]{:S(2)}) %collective-permute-start) | collective-permute-done | bytes 524320 | tf_op jit(solution)/shard_map/ppermute | solution.py:17
  44.4 3.9 collective-permute-start.1
  48.3 22.6 %collective-permute-done.1 = f32[1024,128]{1,0:T(8,128)S(1)} collective-permute-done((f32[1024,128]{1,0:T(8,128)S(1)}, f32[1024,128]{1,0:T(8,128)S(1)}, u32[]{:S(2)}, u32[]{:S(2)}) %collective-permute-start.1) | collective-permute-done | bytes 524320 | tf_op jit(solution)/shard_map/ppermute | solution.py:17
  71.8 6.4 %collective-permute-start.2 = (f32[1024,128]{1,0:T(8,128)S(1)}, f32[1024,128]{1,0:T(8,128)S(1)}, u32[]{:S(2)}, u32[]{:S(2)}) collective-permute-start(f32[1024,128]{1,0:T(8,128)S(1)} %multiply_add_fusion.8), channel_id=1, source_target_pairs={{0,64},{64,0},{16,80},{80,16},{32,96},{96,32},{48,112},{112,48},{1... | collective-permute-start | bytes 1572872 | tf_op jit(solution)/shard_map/ppermute | solution.py:17
  78.2 22.6 %collective-permute-done.2 = f32[1024,128]{1,0:T(8,128)S(1)} collective-permute-done((f32[1024,128]{1,0:T(8,128)S(1)}, f32[1024,128]{1,0:T(8,128)S(1)}, u32[]{:S(2)}, u32[]{:S(2)}) %collective-permute-start.2) | collective-permute-done | bytes 524320 | tf_op jit(solution)/shard_map/ppermute | solution.py:17
  101.6 2.7 collective-permute-start.3
  105.0 9.9 %collective-permute-done.3 = f32[1024,128]{1,0:T(8,128)S(1)} collective-permute-done((f32[1024,128]{1,0:T(8,128)S(1)}, f32[1024,128]{1,0:T(8,128)S(1)}, u32[]{:S(2)}, u32[]{:S(2)}) %collective-permute-start.3) | collective-permute-done | bytes 524320 | tf_op jit(solution)/shard_map/ppermute | solution.py:17
  117.3 8.6 %all-to-all-start = ((f32[64,16,128]{2,0,1:T(8,128)}), f32[64,16,128]{2,0,1:T(8,128)S(1)}, u32[]{:S(2)}, u32[]{:S(2)}) async-start(f32[64,16,128]{2,0,1:T(8,128)} %bitcast.185), calls=%async_computation | async-start | bytes 1048576 | tf_op jit(solution)/shard_map/all_to_all | solution.py:61
  127.3 13.3 %all-to-all-done = f32[64,16,128]{2,0,1:T(8,128)S(1)} async-done(((f32[64,16,128]{2,0,1:T(8,128)}), f32[64,16,128]{2,0,1:T(8,128)S(1)}, u32[]{:S(2)}, u32[]{:S(2)}) %all-to-all-start) | async-done | bytes 524320 | tf_op jit(solution)/shard_map/all_to_all | solution.py:61
  140.6 4.3 %gather_fusion.1 = f32[1024,128]{1,0:T(8,128)} fusion(f32[1024,128]{1,0:T(8,128)S(1)} %bitcast.165, s32[1024]{0:T(1024)} %broadcast_clamp_fusion), kind=kCustom, calls=%fused_computation.1 | custom fusion | bytes 1052672 | tf_op jit(solution)/shard_map/gather | solution.py:64
  145.0 2.0 broadcast_multiply_fusion
  147.9 2.5 gather_fusion.2
  150.5 20.0 %all_to_all.30 = f32[64,16,128]{2,0,1:T(8,128)S(1)} all-to-all(f32[64,16,128]{2,0,1:T(8,128)} %bitcast.186), channel_id=1, replica_groups=mesh['factor'=16,'col'=16] {'factor'}, dimensions={1} | all-to-all | bytes 1048576 | tf_op jit(solution)/shard_map/all_to_all | solution.py:67
  170.4 4.3 %gather_fusion.3 = f32[1024,128]{1,0:T(8,128)} fusion(f32[1024,128]{1,0:T(8,128)S(1)} %bitcast.166, s32[1024]{0:T(1024)} %broadcast_clamp_fusion), kind=kCustom, calls=%fused_computation.3 | custom fusion | bytes 1052672 | tf_op jit(solution)/shard_map/gather | solution.py:70
  174.8 2.6 multiply_reduce_fusion
  177.4 11.4 %collective-permute-done.4 = f32[1024,128]{1,0:T(8,128)S(1)} collective-permute-done((f32[1024,128]{1,0:T(8,128)S(1)}, f32[1024,128]{1,0:T(8,128)S(1)}, u32[]{:S(2)}, u32[]{:S(2)}) %collective-permute-start.4) | collective-permute-done | bytes 524320 | tf_op jit(solution)/shard_map/ppermute | solution.py:17
  190.2 3.2 collective-permute-start.5
  193.5 23.9 %collective-permute-done.5 = f32[1024,128]{1,0:T(8,128)S(1)} collective-permute-done((f32[1024,128]{1,0:T(8,128)S(1)}, f32[1024,128]{1,0:T(8,128)S(1)}, u32[]{:S(2)}, u32[]{:S(2)}) %collective-permute-start.5) | collective-permute-done | bytes 524320 | tf_op jit(solution)/shard_map/ppermute | solution.py:17
  219.0 23.6 %collective-permute-done.6 = f32[1024,128]{1,0:T(8,128)S(1)} collective-permute-done((f32[1024,128]{1,0:T(8,128)S(1)}, f32[1024,128]{1,0:T(8,128)S(1)}, u32[]{:S(2)}, u32[]{:S(2)}) %collective-permute-start.6) | collective-permute-done | bytes 524320 | tf_op jit(solution)/shard_map/ppermute | solution.py:17
  244.4 10.0 %collective-permute-done.7 = f32[1024,128]{1,0:T(8,128)S(1)} collective-permute-done((f32[1024,128]{1,0:T(8,128)S(1)}, f32[1024,128]{1,0:T(8,128)S(1)}, u32[]{:S(2)}, u32[]{:S(2)}) %collective-permute-start.7) | collective-permute-done | bytes 524320 | tf_op jit(solution)/shard_map/ppermute | solution.py:17
  258.5 2.5 fusion.3
  262.0 1.9 rev.78
  266.8 1.9 rev.79
  271.6 2.0 rev.80
  273.6 2.2 fusion.9
  290.4 124.4 %all-reduce.3.cloned.1.call-done = (f32[14,1024]{1,0:T(8,128)}, f32[14,1024]{1,0:T(8,128)}) async-done(((f32[14,1024]{1,0:T(8,128)}, f32[14,1024]{1,0:T(8,128)}), (f32[14,1024]{1,0:T(8,128)}, f32[14,1024]{1,0:T(8,128)})) %all-reduce.3.cloned.1.call-update) | async-done | bytes 114704 | tf_op jit(solution)/shard_map/psum | solution.py:87
  (204 shorter events, 51.6 us)
Async XLA Ops:
  30.4 13.5 %copy-start.8 = (f32[1024,128]{1,0:T(8,128)}, f32[1024,128]{1,0:T(8,128)S(1)}, u32[]{:S(2)}) copy-start(f32[1024,128]{1,0:T(8,128)S(1)} %fusion) | copy-start | bytes 1572868
  30.5 13.2 %copy-start.47 = (f32[1,1024]{1,0:T(1,128)S(1)}, f32[1,1024]{1,0:T(1,128)}, u32[]{:S(2)}) copy-start(f32[1,1024]{1,0:T(1,128)} %get-tuple-element.66) | copy-start | bytes 12292
  30.5 13.1 %collective-permute-start = (f32[1024,128]{1,0:T(8,128)S(1)}, f32[1024,128]{1,0:T(8,128)S(1)}, u32[]{:S(2)}, u32[]{:S(2)}) collective-permute-start(f32[1024,128]{1,0:T(8,128)S(1)} %fusion), channel_id=1, source_target_pairs={{0,16},{16,0},{32,48},{48,32},{64,80},{80,64},{96,112},{112,96},{1... | collective-permute-start | bytes 1572872 | tf_op jit(solution)/shard_map/ppermute | solution.py:17
  44.4 26.9 %copy-start.10 = (f32[1024,128]{1,0:T(8,128)}, f32[1024,128]{1,0:T(8,128)S(1)}, u32[]{:S(2)}) copy-start(f32[1024,128]{1,0:T(8,128)S(1)} %multiply_add_fusion.9) | copy-start | bytes 1572868
  44.4 26.5 %copy-start.51 = (f32[1,1024]{1,0:T(1,128)S(1)}, f32[1,1024]{1,0:T(1,128)}, u32[]{:S(2)}) copy-start(f32[1,1024]{1,0:T(1,128)} %get-tuple-element.65) | copy-start | bytes 12292
  44.4 26.5 %collective-permute-start.1 = (f32[1024,128]{1,0:T(8,128)S(1)}, f32[1024,128]{1,0:T(8,128)S(1)}, u32[]{:S(2)}, u32[]{:S(2)}) collective-permute-start(f32[1024,128]{1,0:T(8,128)S(1)} %multiply_add_fusion.9), channel_id=1, source_target_pairs={{0,32},{32,0},{16,48},{48,16},{64,96},{96,64},{80,112},{112,80},{1... | collective-permute-start | bytes 1572872 | tf_op jit(solution)/shard_map/ppermute | solution.py:17
  70.9 29.9 %copy-start.55 = (f32[1,1024]{1,0:T(1,128)S(1)}, f32[1,1024]{1,0:T(1,128)}, u32[]{:S(2)}) copy-start(f32[1,1024]{1,0:T(1,128)} %get-tuple-element.64) | copy-start | bytes 12292
  71.7 29.4 %copy-start.12 = (f32[1024,128]{1,0:T(8,128)}, f32[1024,128]{1,0:T(8,128)S(1)}, u32[]{:S(2)}) copy-start(f32[1024,128]{1,0:T(8,128)S(1)} %multiply_add_fusion.8) | copy-start | bytes 1572868
  71.8 29.0 %copy-start.49 = (f32[1,1024]{1,0:T(1,128)S(1)}, f32[1,1024]{1,0:T(1,128)}, u32[]{:S(2)}) copy-start(f32[1,1024]{1,0:T(1,128)} %get-tuple-element.50) | copy-start | bytes 12292
  71.8 29.0 %collective-permute-start.2 = (f32[1024,128]{1,0:T(8,128)S(1)}, f32[1024,128]{1,0:T(8,128)S(1)}, u32[]{:S(2)}, u32[]{:S(2)}) collective-permute-start(f32[1024,128]{1,0:T(8,128)S(1)} %multiply_add_fusion.8), channel_id=1, source_target_pairs={{0,64},{64,0},{16,80},{80,16},{32,96},{96,32},{48,112},{112,48},{1... | collective-permute-start | bytes 1572872 | tf_op jit(solution)/shard_map/ppermute | solution.py:17
  101.6 13.6 %copy-start.31 = (f32[1024,128]{1,0:T(8,128)}, f32[1024,128]{1,0:T(8,128)S(1)}, u32[]{:S(2)}) copy-start(f32[1024,128]{1,0:T(8,128)S(1)} %multiply_add_fusion.7) | copy-start | bytes 1572868
  101.6 13.2 %collective-permute-start.3 = (f32[1024,128]{1,0:T(8,128)S(1)}, f32[1024,128]{1,0:T(8,128)S(1)}, u32[]{:S(2)}, u32[]{:S(2)}) collective-permute-start(f32[1024,128]{1,0:T(8,128)S(1)} %multiply_add_fusion.7), channel_id=1, source_target_pairs={{0,128},{128,0},{16,144},{144,16},{32,160},{160,32},{48,176},{176,... | collective-permute-start | bytes 1572872 | tf_op jit(solution)/shard_map/ppermute | solution.py:17
  104.4 10.5 %copy-start.57 = (f32[1,1024]{1,0:T(1,128)S(1)}, f32[1,1024]{1,0:T(1,128)}, u32[]{:S(2)}) copy-start(f32[1,1024]{1,0:T(1,128)} %get-tuple-element.63) | copy-start | bytes 12292
  105.0 9.9 %copy-start.53 = (f32[1,1024]{1,0:T(1,128)S(1)}, f32[1,1024]{1,0:T(1,128)}, u32[]{:S(2)}) copy-start(f32[1,1024]{1,0:T(1,128)} %get-tuple-element.49) | copy-start | bytes 12292
  117.3 23.3 %all-to-all-start = ((f32[64,16,128]{2,0,1:T(8,128)}), f32[64,16,128]{2,0,1:T(8,128)S(1)}, u32[]{:S(2)}, u32[]{:S(2)}) async-start(f32[64,16,128]{2,0,1:T(8,128)} %bitcast.185), calls=%async_computation | async-start | bytes 1048576 | tf_op jit(solution)/shard_map/all_to_all | solution.py:61
  126.0 288.8 %all-reduce.3.cloned.1.call-start = ((), (), s32[]{:S(2)}) async-start(), calls=%async_computation.2 | async-start | bytes 262144 | tf_op jit(solution)/shard_map/psum | solution.py:87
  174.8 14.1 %copy-start.13 = (f32[1024,128]{1,0:T(8,128)S(1)}, f32[1024,128]{1,0:T(8,128)}, u32[]{:S(2)}) copy-start(f32[1024,128]{1,0:T(8,128)} %copy-done.12) | copy-start | bytes 1572868
  174.8 14.1 %copy-start.36 = (f32[1024,128]{1,0:T(8,128)S(1)}, f32[1024,128]{1,0:T(8,128)}, u32[]{:S(2)}) copy-start(f32[1024,128]{1,0:T(8,128)} %gather_fusion.3) | copy-start | bytes 1572868
  174.8 14.1 %copy-start.43 = (f32[1024,128]{1,0:T(8,128)S(1)}, f32[1024,128]{1,0:T(8,128)}, u32[]{:S(2)}) copy-start(f32[1024,128]{1,0:T(8,128)} %copy-done.42) | copy-start | bytes 1572868
  174.8 14.1 %copy-start.54 = (f32[1,1024]{1,0:T(1,128)S(1)}, f32[1,1024]{1,0:T(1,128)}, u32[]{:S(2)}) copy-start(f32[1,1024]{1,0:T(1,128)} %get-tuple-element.49) | copy-start | bytes 12292
  177.4 11.5 %collective-permute-start.4 = (f32[1024,128]{1,0:T(8,128)S(1)}, f32[1024,128]{1,0:T(8,128)S(1)}, u32[]{:S(2)}, u32[]{:S(2)}) collective-permute-start(f32[1024,128]{1,0:T(8,128)S(1)} %get-tuple-element.48), channel_id=1, source_target_pairs={{0,128},{128,0},{16,144},{144,16},{32,160},{160,32},{48,176},{176,... | collective-permute-start | bytes 1572872 | tf_op jit(solution)/shard_map/ppermute | solution.py:17
  190.0 27.3 %copy-start.11 = (f32[1024,128]{1,0:T(8,128)S(1)}, f32[1024,128]{1,0:T(8,128)}, u32[]{:S(2)}) copy-start(f32[1024,128]{1,0:T(8,128)} %copy-done.10) | copy-start | bytes 1572868
  190.0 27.3 %copy-start.41 = (f32[1024,128]{1,0:T(8,128)S(1)}, f32[1024,128]{1,0:T(8,128)}, u32[]{:S(2)}) copy-start(f32[1024,128]{1,0:T(8,128)} %copy-done.40) | copy-start | bytes 1572868
  190.0 27.3 %copy-start.50 = (f32[1,1024]{1,0:T(1,128)S(1)}, f32[1,1024]{1,0:T(1,128)}, u32[]{:S(2)}) copy-start(f32[1,1024]{1,0:T(1,128)} %get-tuple-element.50) | copy-start | bytes 12292
  190.2 27.1 %collective-permute-start.5 = (f32[1024,128]{1,0:T(8,128)S(1)}, f32[1024,128]{1,0:T(8,128)S(1)}, u32[]{:S(2)}, u32[]{:S(2)}) collective-permute-start(f32[1024,128]{1,0:T(8,128)S(1)} %broadcast_multiply_fusion.2), channel_id=1, source_target_pairs={{0,64},{64,0},{16,80},{80,16},{32,96},{96,32},{48,112},{112,48},{1... | collective-permute-start | bytes 1572872 | tf_op jit(solution)/shard_map/ppermute | solution.py:17
  218.5 24.1 %copy-start.9 = (f32[1024,128]{1,0:T(8,128)S(1)}, f32[1024,128]{1,0:T(8,128)}, u32[]{:S(2)}) copy-start(f32[1024,128]{1,0:T(8,128)} %copy-done.8) | copy-start | bytes 1572868
  218.5 24.1 %copy-start.39 = (f32[1024,128]{1,0:T(8,128)S(1)}, f32[1024,128]{1,0:T(8,128)}, u32[]{:S(2)}) copy-start(f32[1024,128]{1,0:T(8,128)} %copy-done.38) | copy-start | bytes 1572868
  218.7 23.8 %collective-permute-start.6 = (f32[1024,128]{1,0:T(8,128)S(1)}, f32[1024,128]{1,0:T(8,128)S(1)}, u32[]{:S(2)}, u32[]{:S(2)}) collective-permute-start(f32[1024,128]{1,0:T(8,128)S(1)} %broadcast_multiply_fusion.3), channel_id=1, source_target_pairs={{0,32},{32,0},{16,48},{48,16},{64,96},{96,64},{80,112},{112,80},{1... | collective-permute-start | bytes 1572872 | tf_op jit(solution)/shard_map/ppermute | solution.py:17
  243.6 10.8 %copy-start.5 = (f32[1024,128]{1,0:T(8,128)S(1)}, f32[1024,128]{1,0:T(8,128)}, u32[]{:S(2)}) copy-start(f32[1024,128]{1,0:T(8,128)} %fusion.2) | copy-start | bytes 1572868
  243.6 10.8 %copy-start.23 = (f32[1,2,512,128]{3,2,1,0:T(8,128)S(1)}, f32[1,2,512,128]{3,2,1,0:T(8,128)}, u32[]{:S(2)}) copy-start(f32[1,2,512,128]{3,2,1,0:T(8,128)} %rev.76) | copy-start | bytes 1572868
  243.8 10.6 %collective-permute-start.7 = (f32[1024,128]{1,0:T(8,128)S(1)}, f32[1024,128]{1,0:T(8,128)S(1)}, u32[]{:S(2)}, u32[]{:S(2)}) collective-permute-start(f32[1024,128]{1,0:T(8,128)S(1)} %broadcast_multiply_fusion.4), channel_id=1, source_target_pairs={{0,16},{16,0},{32,48},{48,32},{64,80},{80,64},{96,112},{112,96},{1... | collective-permute-start | bytes 1572872 | tf_op jit(solution)/shard_map/ppermute | solution.py:17
  290.4 124.4 %copy-start.46 = (f32[14,1024]{1,0:T(8,128)S(1)}, f32[14,1024]{1,0:T(8,128)}, u32[]{:S(2)}) copy-start(f32[14,1024]{1,0:T(8,128)} %param.13) | copy-start | bytes 172036
  (49 other events, 59.2 us)
Sparse Core Ops, SparseCore 0:
  290.5 124.2 all-reduce.2
where the time goes:
time: 425 us; the launch traced here: 423 us
  waiting for transfers between devices  272 us (64%)
  local copies, waits for them, and re-layouts  46.9 us (11%)
  other arithmetic  40.8 us (10%)
  starting transfers between devices  28.5 us (7%)
  blocking collectives  20 us (5%)
  between operations  14.6 us (3%)
    ppermute x8, waiting for transfers between devices, partner(): return lax.ppermute(block, axis, route)  135 us
    psum x1, waiting for transfers between devices, per_device(): grad_diag, grad_cross = lax.psum((grad_diag, grad_cross), 'col')  124 us
    all_to_all x1, blocking collectives, per_device(): lax.all_to_all(to_owner(scaled, groups), 'factor', split_axis=1, concat_a...  20 us
    ppermute x8, starting transfers between devices, partner(): return lax.ppermute(block, axis, route)  19.8 us
    reduce_sum x13, other arithmetic, per_device(): cross_terms[level] = jnp.sum(gradient * beside, axis=1)  19.2 us
    rev x19, local copies, waits for them, and re-layouts, partner_rows(): return jnp.flip(folded, 1).reshape(values.shape)  17.5 us
    all_to_all x1, waiting for transfers between devices, per_device(): lax.all_to_all(to_owner(field, groups), 'factor', split_axis=1, concat_ax...  13.3 us
    unnamed x142, local copies, waits for them, and re-layouts  10.5 us
  transfers between devices with their start and end apart: 10, of which 10 were waited for; matrix products, arithmetic and copies ran while one was open for 0% of the time, Pallas kernels for 0%

commit v1 on v0

v1 whole, which is shorter than its diff:
```python
import functools

import jax
import jax.numpy as jnp
from jax import lax
from jax.experimental import pallas as pl
from jax.experimental.pallas import tpu as pltpu
from jax.sharding import PartitionSpec as P

MESH = pl.DeviceIdType.MESH
F32, BF16 = jnp.float32, jnp.bfloat16
step_scale = 0.03
TOKENS = 2048


def bit(value, place):
    return lax.rem(lax.div(value, 2**place), 2)


def rev3(v):
    return bit(v, 0) * 4 + bit(v, 1) * 2 + bit(v, 2)


def rev4(v):
    return bit(v, 0) * 8 + bit(v, 1) * 4 + bit(v, 2) * 2 + bit(v, 3)


def rev_const(v, bits):
    return int(format(v, "0%db" % bits)[::-1], 2)


def flip(value, place):
    return value + 2**place - 2 ** (place + 1) * bit(value, place)


def forward_pairs(x, span, diag, cross):
    out = list(x)
    for i in range(len(x)):
        out[i] = diag(i) * x[i] + cross(i) * x[i ^ span]
    return out


def backward_pairs(b, span, diag, cross):
    carried = [cross(i) * b[i] for i in range(len(b))]
    return [diag(i) * b[i] + carried[i ^ span] for i in range(len(b))]


def loop(count, body):
    def step(j, carry):
        body(j)
        return carry

    lax.fori_loop(0, count, step, 0)


def lane_sums(pairs):
    rows = lax.broadcasted_iota(jnp.int32, (16, 128), 0)
    total = None
    for level, (first, second) in enumerate(pairs):
        ones = jnp.where(rows == level, 1.0, 0.0).astype(BF16)
        block = jnp.concatenate([first, second], axis=0)
        high = block.astype(BF16)
        low = (block - high.astype(F32)).astype(BF16)
        for part in (high, low):
            term = lax.dot_general(ones, part, (((1,), (1,)), ((), ())), preferred_element_type=F32)
            total = term if total is None else total + term
    return total


def swap_tiles(block, span):
    tiles = [block[8 * k : 8 * k + 8] for k in range(8)]
    return jnp.concatenate([tiles[k ^ span] for k in range(8)], axis=0)


def kernel(
    act, tgt, dg, cr,
    nd, nc, res,
    xs, ts, wst, wt, wts, wz, wmsg, wbin, wtb,
    wa, wb, fa, ba, fb, bb,
    inb, outb, ina, ga, gb, gpart, gsum, rs, ot, pt,
    s1, r1, s2, r2, s3, r3, s4, r4, s5, r5, s6, r6,
):
    me = lax.axis_index("factor")
    col = lax.axis_index("col")
    mx, mz = lax.div(me, 8), lax.rem(me, 8)

    barrier = pltpu.get_barrier_semaphore()

    def greet(j):
        pl.semaphore_signal(
            barrier, inc=1, device_id={"factor": lax.rem(me + 1 + j, 16)}, device_id_type=MESH
        )
        pl.semaphore_signal(
            barrier, inc=1, device_id={"col": lax.rem(col + 1 + j, 16)}, device_id_type=MESH
        )

    loop(15, greet)

    def peer(j, sign):
        dx = 1 - lax.div(j, 8)
        dz = lax.rem(dx * (j + 4) + (1 - dx) * (j - 7), 8)
        return lax.rem(mx + dx, 2) * 8 + lax.rem(mz + sign * dz + 8, 8)

    wst[...] = jnp.zeros_like(wst)
    for s in range(14):
        row = s + (s >= 7)
        wst[row : row + 1, :] = dg[s : s + 1, :]
        wst[16 + row : 17 + row, :] = cr[s : s + 1, :]
    for k in range(8):
        wt[128 * k : 128 * k + 128, :] = wst[:, 128 * k : 128 * k + 128].T

    def spread_a(u):
        t = rev3(u)
        here = pl.ds(8 * u, 8)
        for a in range(16):
            tile = wt[pl.ds(16 * t + a, 8, stride=128), :]
            wts[a, here, :] = tile
            for s in range(7):
                wa[0, s, a, here, :] = jnp.broadcast_to(tile[:, s : s + 1], (8, 128))
                wa[1, s, a, here, :] = jnp.broadcast_to(tile[:, 16 + s : 17 + s], (8, 128))

    loop(8, spread_a)

    lane = lax.broadcasted_iota(jnp.int32, (8, 128), 1)

    def pack_b(p):
        for kind in range(2):
            packed = jnp.zeros((8, 128), F32)
            for a in range(16):
                tile = wts[a, pl.ds(p, 8, stride=8), :]
                moved = pltpu.roll(tile, (8 * a - 8 - 16 * kind) % 128, axis=1)
                packed = jnp.where(lax.div(lane, 8) == a, moved, packed)
            wz[pl.ds(64 * kind + 8 * p, 8), :] = packed

    loop(8, pack_b)
    wmsg[...] = wz[...].T.reshape(16, 8, 128)

    def convert(j):
        here = pl.ds(16 * j, 16)
        xs[here, :] = act[here, :].astype(F32)
        ts[here, :] = tgt[here, :].astype(F32)

    loop(64, convert)

    def forward_a(u):
        t = rev3(u)
        here = pl.ds(8 * u, 8)
        x = [xs[pl.ds(16 * t + a, 8, stride=128), :] for a in range(16)]
        for s in range(4):
            for a in range(16):
                fa[s, a, here, :] = x[a]
            x = forward_pairs(x, 2**s, lambda a: wa[0, s, a, here, :], lambda a: wa[1, s, a, here, :])
        for a in range(16):
            fa[4, a, here, :] = x[a]

    loop(8, forward_a)

    def tile(k):
        return slice(8 * k, 8 * k + 8)

    def finish_a(a, target, index):
        x = [fa[4, a, tile(u), :] for u in range(8)]
        for s in range(4, 7):
            if s > 4:
                for u in range(8):
                    fa[s, a, tile(u), :] = x[u]
            x = forward_pairs(
                x, 2 ** (6 - s), lambda u: wa[0, s, a, tile(u), :], lambda u: wa[1, s, a, tile(u), :]
            )
        for u in range(8):
            target[index, tile(u), :] = x[u]

    pl.semaphore_wait(barrier, 30)

    def copy_w(g):
        return pltpu.make_async_remote_copy(
            src_ref=wmsg.at[rev4(g)], dst_ref=wbin.at[me], send_sem=s1.at[g], recv_sem=r1.at[me],
            device_id={"factor": g}, device_id_type=MESH,
        )

    def copy_x(g):
        return pltpu.make_async_remote_copy(
            src_ref=outb.at[rev4(g)], dst_ref=inb.at[me], send_sem=s2.at[g], recv_sem=r2.at[me],
            device_id={"factor": g}, device_id_type=MESH,
        )

    def landed(buffer, sems, source):
        return pltpu.make_async_remote_copy(
            src_ref=buffer.at[source], dst_ref=buffer.at[source], send_sem=sems.at[source], recv_sem=sems.at[source],
            device_id={"factor": source}, device_id_type=MESH,
        ).wait_recv()

    def send_a(j):
        g = peer(j, 1)
        copy_w(g).start()
        finish_a(rev4(g), outb, rev4(g))
        copy_x(g).start()

    loop(15, send_a)
    finish_a(rev4(me), inb, me)
    wbin[me] = wmsg[rev4(me)]

    loop(15, lambda j: landed(wbin, r1, peer(j, -1)))
    wtb[...] = wbin[...].reshape(128, 128).T

    def spread_b(p):
        here = pl.ds(8 * p, 8)
        diag = wtb[here, :]
        cross = wtb[pl.ds(64 + 8 * p, 8), :]
        for f in range(16):
            for s in range(7):
                k = 8 * f + s
                wb[0, s, f, here, :] = jnp.broadcast_to(diag[:, k : k + 1], (8, 128))
                wb[1, s, f, here, :] = jnp.broadcast_to(cross[:, k : k + 1], (8, 128))

    loop(8, spread_b)

    def forward_b(f):
        x = [inb[f, pl.ds(p, 8, stride=8), :] for p in range(8)]
        for s in range(3):
            for p in range(8):
                fb[s, f, tile(p), :] = x[p]
            x = forward_pairs(x, 2**s, lambda p: wb[0, s, f, tile(p), :], lambda p: wb[1, s, f, tile(p), :])
        for p in range(8):
            fb[3, f, tile(p), :] = x[p]

    forward_b(me)

    def arrive_b(j):
        f = peer(14 - j, -1)
        landed(inb, r2, f)
        forward_b(f)

    loop(15, arrive_b)

    def turn(p):
        here = pl.ds(8 * p, 8)
        x = [fb[3, f, here, :] for f in range(16)]
        for s in range(3, 7):
            if s > 3:
                for f in range(16):
                    fb[s, f, here, :] = x[f]
            x = forward_pairs(x, 2 ** (s - 3), lambda f: wb[0, s, f, here, :], lambda f: wb[1, s, f, here, :])
        b = []
        for f in range(16):
            rows = pl.ds(rev3(p) * 16 + rev_const(f, 4), 8, stride=128)
            error = x[f] - ts[rows, :]
            res[rows, :] = error
            b.append((2.0 / TOKENS) * error)
        for s in range(6, 2, -1):
            for f in range(16):
                bb[s, f, here, :] = b[f]
            b = backward_pairs(b, 2 ** (s - 3), lambda f: wb[0, s, f, here, :], lambda f: wb[1, s, f, here, :])
        for f in range(16):
            bb[2, f, here, :] = b[f]

    loop(8, turn)

    def backward_b(f, target, index):
        b = [bb[2, f, tile(p), :] for p in range(8)]
        for s in range(2, -1, -1):
            if s < 2:
                for p in range(8):
                    bb[s, f, tile(p), :] = b[p]
            b = backward_pairs(b, 2**s, lambda p: wb[0, s, f, tile(p), :], lambda p: wb[1, s, f, tile(p), :])
        for p in range(8):
            target[index, pl.ds(p, 8, stride=8), :] = b[p]

    loop(15, lambda j: copy_x(peer(j, 1)).wait_send())
    mine = rev4(me)

    def copy_b(f):
        return pltpu.make_async_remote_copy(
            src_ref=outb.at[f], dst_ref=ina.at[mine], send_sem=s3.at[f], recv_sem=r3.at[mine],
            device_id={"factor": f}, device_id_type=MESH,
        )

    def send_b(j):
        f = peer(j, 1)
        backward_b(f, outb, f)
        copy_b(f).start()

    loop(15, send_b)
    backward_b(me, ina, mine)

    def grads_b(f):
        pairs = []
        for s in range(7):
            back = bb[s, f]
            own = fb[s, f]
            other = swap_tiles(own, 2**s) if s < 3 else fb[s, flip(f, s - 3)]
            pairs.append((back * own, back * other))
        return lane_sums(pairs)[0:8]

    def copy_g(f):
        return pltpu.make_async_remote_copy(
            src_ref=gb.at[f], dst_ref=gpart.at[1, mine], send_sem=s4.at[f], recv_sem=r4.at[mine],
            device_id={"factor": f}, device_id_type=MESH,
        )

    def send_g(j):
        f = peer(j, 1)
        gb[f] = grads_b(f)
        copy_g(f).start()

    loop(15, send_g)
    gpart[1, mine] = grads_b(me)

    def backward_a(a):
        b = [ina[a, tile(u), :] for u in range(8)]
        for s in range(6, 3, -1):
            for u in range(8):
                ba[s, a, tile(u), :] = b[u]
            b = backward_pairs(
                b, 2 ** (6 - s), lambda u: wa[0, s, a, tile(u), :], lambda u: wa[1, s, a, tile(u), :]
            )
        for u in range(8):
            ba[3, a, tile(u), :] = b[u]

    backward_a(mine)

    def arrive_a(j):
        g = peer(14 - j, -1)
        a = rev4(g)
        landed(ina, r3, a)
        backward_a(a)

    loop(15, arrive_a)

    def last_a(u):
        here = pl.ds(8 * u, 8)
        b = [ba[3, a, here, :] for a in range(16)]
        for s in range(3, 0, -1):
            b = backward_pairs(b, 2**s, lambda a: wa[0, s, a, here, :], lambda a: wa[1, s, a, here, :])
            for a in range(16):
                ba[s - 1, a, here, :] = b[a]

    loop(8, last_a)

    def grads_a(a):
        pairs = []
        for s in range(7):
            back = ba[s, a]
            own = fa[s, a]
            other = fa[s, flip(a, s)] if s < 4 else swap_tiles(own, 2 ** (6 - s))
            pairs.append((back * own, back * other))
        gpart[0, a] = lane_sums(pairs)[0:8]

    loop(16, grads_a)

    def landed_g(j):
        a = rev4(peer(j, -1))
        pltpu.make_async_remote_copy(
            src_ref=gb.at[a], dst_ref=gpart.at[1, a], send_sem=s4.at[a], recv_sem=r4.at[a],
            device_id={"factor": me}, device_id_type=MESH,
        ).wait_recv()

    loop(15, landed_g)

    def copy_r(c):
        return pltpu.make_async_remote_copy(
            src_ref=gpart.at[:, c], dst_ref=rs.at[col], send_sem=s5.at[c], recv_sem=r5.at[col],
            device_id={"col": c}, device_id_type=MESH,
        )

    def col_landed(buffer, sems, source):
        pltpu.make_async_remote_copy(
            src_ref=buffer, dst_ref=buffer, send_sem=sems.at[source], recv_sem=sems.at[source],
            device_id={"col": source}, device_id_type=MESH,
        ).wait_recv()

    loop(15, lambda j: copy_r(lax.rem(col + 1 + j, 16)).start())
    rs[col] = gpart[:, col]
    loop(15, lambda j: col_landed(rs.at[lax.rem(col + 15 - j, 16)], r5, lax.rem(col + 15 - j, 16)))
    summed = rs[0]
    for c in range(1, 16):
        summed = summed + rs[c]
    gsum[:, col] = summed

    def copy_s(c):
        return pltpu.make_async_remote_copy(
            src_ref=gsum.at[:, col], dst_ref=gsum.at[:, col], send_sem=s6.at[c], recv_sem=r6.at[col],
            device_id={"col": c}, device_id_type=MESH,
        )

    loop(15, lambda j: copy_s(lax.rem(col + 1 + j, 16)).start())
    loop(15, lambda j: col_landed(gsum.at[:, lax.rem(col + 15 - j, 16)], r6, lax.rem(col + 15 - j, 16)))

    pt[0] = gsum[0].reshape(128, 128).T
    pt[1] = gsum[1].reshape(128, 128).T

    def unpack(u):
        t = rev3(u)
        parts = []
        for kind in range(2):
            parts.append(pt[0, pl.ds(64 * kind + 8 * u, 8), :])
            parts.append(pt[1, pl.ds(64 * kind + u, 8, stride=8), :])
        for a in range(16):
            row = jnp.zeros((8, 128), F32)
            for k in range(4):
                row = jnp.where(lax.div(lane, 8) == k, pltpu.roll(parts[k], (8 * k - 8 * a) % 128, axis=1), row)
            ot[pl.ds(16 * t + a, 8, stride=128), :] = row

    loop(8, unpack)
    for k in range(8):
        here = slice(128 * k, 128 * k + 128)
        wst[:, here] = ot[here, :].T
    for s in range(14):
        row = s + (s >= 7)
        nd[s : s + 1, :] = dg[s : s + 1, :] - step_scale * wst[row : row + 1, :]
        nc[s : s + 1, :] = cr[s : s + 1, :] - step_scale * wst[16 + row : 17 + row, :]

    def drain(j):
        g = peer(j, 1)
        copy_w(g).wait_send()
        copy_b(g).wait_send()
        copy_g(g).wait_send()
        c = lax.rem(col + 1 + j, 16)
        copy_r(c).wait_send()
        copy_s(c).wait_send()

    loop(15, drain)


def per_device(activations, targets, diagonal, crossing):
    height, width = activations.shape
    big = lambda *lead: pltpu.VMEM(lead + (16, 64, 128), F32)
    plain = lambda *shape: pltpu.VMEM(shape, F32)
    return pl.pallas_call(
        kernel,
        out_shape=(
            jax.ShapeDtypeStruct(diagonal.shape, F32),
            jax.ShapeDtypeStruct(crossing.shape, F32),
            jax.ShapeDtypeStruct((height, width), F32),
        ),
        in_specs=[pl.BlockSpec(memory_space=pltpu.VMEM)] * 4,
        out_specs=(pl.BlockSpec(memory_space=pltpu.VMEM),) * 3,
        scratch_shapes=[
            plain(1024, 128), plain(1024, 128), plain(128, 1024), plain(1024, 128), plain(16, 64, 128),
            plain(128, 128), plain(16, 8, 128), plain(16, 8, 128), plain(128, 128),
            big(2, 7), big(2, 7), big(7), big(7), big(7), big(7),
            big(), big(), big(), plain(16, 8, 128), plain(16, 8, 128),
            plain(2, 16, 8, 128), plain(2, 16, 8, 128), plain(16, 2, 8, 128), plain(1024, 128), plain(2, 128, 128),
        ]
        + [pltpu.SemaphoreType.DMA((16,))] * 12,
        compiler_params=pltpu.CompilerParams(
            collective_id=0, has_side_effects=True, vmem_limit_bytes=56 * 2**20
        ),
    )(activations, targets, diagonal, crossing)


def solution(mesh):
    placed = (P("factor", "col"), P("factor", "col"), P(None, "factor"), P(None, "factor"))
    return jax.shard_map(
        per_device,
        mesh=mesh,
        in_specs=placed,
        out_specs=(P(None, "factor"), P(None, "factor"), P("factor", "col")),
        check_vma=False,
    )
```

time: 425 us -> 73.3 us (0.17)
  waiting for transfers between devices: 272 us -> 0 us
  Pallas kernels: 0 us -> 68.5 us
  local copies, waits for them, and re-layouts: 46.9 us -> 4.01 us
  other arithmetic: 40.8 us -> 0 us
  starting transfers between devices: 28.5 us -> 0 us
  blocking collectives: 20 us -> 0 us
  between operations: 14.6 us -> 0.65 us
    ppermute x8 -> x0, waiting for transfers between devices: 135 us -> none  [partner(): return lax.ppermute(block, axis, route)]
    psum x1 -> x0, waiting for transfers between devices: 124 us -> none  [per_device(): grad_diag, grad_cross = lax.psum((grad_diag, grad_cross), 'col')]
    pallas_call x0 -> x1, Pallas kernels: none -> 68.5 us  [per_device(): pl.pallas_call(kernel, out_shape=(jax.ShapeDtypeStruct(diagonal.shape, F3...]
    all_to_all x1 -> x0, blocking collectives: 20 us -> none  [per_device(): lax.all_to_all(to_owner(scaled, groups), 'factor', split_axis=1, concat_a...]
    ppermute x8 -> x0, starting transfers between devices: 19.8 us -> none  [partner(): return lax.ppermute(block, axis, route)]
    reduce_sum x13 -> x0, other arithmetic: 19.2 us -> none  [per_device(): cross_terms[level] = jnp.sum(gradient * beside, axis=1)]
    rev x19 -> x0, local copies, waits for them, and re-layouts: 17.5 us -> none  [partner_rows(): return jnp.flip(folded, 1).reshape(values.shape)]
    all_to_all x1 -> x0, waiting for transfers between devices: 13.3 us -> none  [per_device(): lax.all_to_all(to_owner(field, groups), 'factor', split_axis=1, concat_ax...]
  transfers between devices with their start and end apart: 10 -> 0, of which waited for: 10 -> 0; matrix products, arithmetic and copies ran while one was open for 0% -> 0% of each run, Pallas kernels for 0% -> 0%
where the time goes in v1:
time: 73.3 us; the launch traced here: 73.1 us
  Pallas kernels  68.5 us (93%)
  local copies, waits for them, and re-layouts  4.01 us (5%)
    pallas_call x1, Pallas kernels, per_device(): pl.pallas_call(kernel, out_shape=(jax.ShapeDtypeStruct(diagonal.shape, F3...  68.5 us
    unnamed x5, local copies, waits for them, and re-layouts  4.01 us

profile of v1, /device:TPU:1, one launch (start us, length us, event | category | flops | bytes accessed | tf_op | source)
XLA Modules:
  0.0 73.1 jit_solution(10047474599534615591)
XLA Ops:
  0.6 68.5 %shard_map.67 = (f32[14,1024]{1,0:T(8,128)}, f32[14,1024]{1,0:T(8,128)}, f32[1024,128]{1,0:T(8,128)}) custom-call(bf16[1024,128]{1,0:T(8,128)(2,1)} %act.1, bf16[1024,128]{1,0:T(8,128)(2,1)} %tgt.1, f32[14,1024]{1,0:T(8,128)} %dg.1, f32[14,1024]{1,0:T(8,128)} %cr.1), custom_call_target="tpu_custom_call" | custom-call | tf_op jit(solution)/shard_map/pallas_call | solution.py:429
  69.1 0.0 copy-start
  69.1 1.5 %copy.10 = f32[14,1024]{1,0:T(8,128)} copy(f32[14,1024]{1,0:T(8,128)} %get-tuple-element.6) | data formatting | bytes 114688
  70.6 0.0 copy-done
  70.6 0.6 copy.11
  71.3 1.9 %copy.12 = f32[1024,128]{1,0:T(8,128)} copy(f32[1024,128]{1,0:T(8,128)} %get-tuple-element.8) | data formatting | bytes 1048576
Async XLA Ops:
  69.1 1.5 %copy-start = (f32[14,1024]{1,0:T(8,128)S(1)}, f32[14,1024]{1,0:T(8,128)}, u32[]{:S(2)}) copy-start(f32[14,1024]{1,0:T(8,128)} %get-tuple-element.7) | copy-start | bytes 172036

commit v2 on v0

v2 whole, which is shorter than its diff:
```python
import jax
import jax.numpy as jnp
from jax import lax
from jax.experimental import pallas as pl
from jax.experimental.pallas import tpu as pltpu
from jax.sharding import PartitionSpec as P

MESH = pl.DeviceIdType.MESH
F32, BF16 = jnp.float32, jnp.bfloat16
step_scale = 0.03
TOKENS = 2048
PARTS = 4
UP = 8 // PARTS


def bit(value, place):
    return lax.rem(lax.div(value, 2**place), 2)


def rev3(v):
    return bit(v, 0) * 4 + bit(v, 1) * 2 + bit(v, 2)


def rev4(v):
    return bit(v, 0) * 8 + bit(v, 1) * 4 + bit(v, 2) * 2 + bit(v, 3)


def rev_const(v, bits):
    return int(format(v, "0%db" % bits)[::-1], 2)


def slot(s):
    return s + (s >= 3)


def forward_pairs(x, span, diag, cross):
    return [diag(i) * x[i] + cross(i) * x[i ^ span] for i in range(len(x))]


def backward_pairs(b, span, diag, cross):
    carried = [cross(i) * b[i] for i in range(len(b))]
    return [diag(i) * b[i] + carried[i ^ span] for i in range(len(b))]


def loop(count, body):
    def step(j, carry):
        body(j)
        return carry

    lax.fori_loop(0, count, step, 0)


def thirds(value):
    high = value.astype(BF16).astype(F32)
    rest = value - high
    middle = rest.astype(BF16).astype(F32)
    return high, middle, rest - middle


def kernel(
    act_hbm, tgt_hbm, dg_hbm, cr_hbm,
    nd, nc, res,
    act, tgt, dg, cr,
    xs, ts, es, wst, wt, wtb16, ebc, wz, wmsg, wbin, wtb,
    wa, w1, w2, fa, b5, f1, f2, b1, b2,
    outa, inb, outb, ina, parta, partb, gz, gt, gin, gpart, rs, gs, gout,
    ld, s1, r1, s2, r2, s3, r3, s4, r4, s5, r5, s6, r6,
):
    me = lax.axis_index("factor")
    col = lax.axis_index("col")
    mx, mz = lax.div(me, 8), lax.rem(me, 8)
    mine = rev4(me)

    loads = [
        pltpu.make_async_copy(a, b, ld.at[k])
        for k, (a, b) in enumerate([(dg_hbm, dg), (cr_hbm, cr), (act_hbm, act), (tgt_hbm, tgt)])
    ]
    for copy in loads:
        copy.start()

    barrier = pltpu.get_barrier_semaphore()

    def greet(j):
        pl.semaphore_signal(
            barrier, inc=1, device_id={"factor": lax.rem(me + 1 + j, 16)}, device_id_type=MESH
        )
        pl.semaphore_signal(
            barrier, inc=1, device_id={"col": lax.rem(col + 1 + j, 16)}, device_id_type=MESH
        )

    loop(15, greet)

    def peer(j, sign):
        dx = 1 - lax.div(j, 8)
        dz = lax.rem(dx * (j + 4) + (1 - dx) * (j - 7), 8)
        return lax.rem(mx + dx, 2) * 8 + lax.rem(mz + sign * dz + 8, 8)

    lane = lax.broadcasted_iota(jnp.int32, (8, 128), 1)
    lane_low = [lax.rem(lax.div(lane, 2**k), 2) == 0 for k in range(7)]

    def choose(tiles):
        k = 3
        while len(tiles) > 1:
            tiles = [jnp.where(lane_low[k], tiles[i], tiles[i + 1]) for i in range(0, len(tiles), 2)]
            k += 1
        return tiles[0]

    def lane_sums(blocks, n):
        block = jnp.concatenate(blocks, axis=0)
        high = block.astype(BF16)
        low = (block - high.astype(F32)).astype(BF16)
        return jnp.dot(jnp.concatenate([high, low], axis=1), ebc[n], preferred_element_type=F32)

    def tiles_of(block, k):
        return [block[128 * k + 8 * i : 128 * k + 8 * i + 8] for i in range(16)]

    wst[96:128, :] = jnp.zeros((32, 1024), F32)
    loads[0].wait()
    loads[1].wait()
    for s in range(14):
        row = 96 + (s if s < 7 else 8 + slot(s - 7))
        wst[row : row + 1, :] = dg[s : s + 1, :]
        wst[16 + row : 17 + row, :] = cr[s : s + 1, :]
    high, middle, rest = thirds(wst[96:128, :])
    wst[0:32, :] = high
    wst[32:64, :] = middle
    wst[64:96, :] = rest
    for k in range(8):
        wt[128 * k : 128 * k + 128, :] = wst[:, 128 * k : 128 * k + 128].T

    def gather_a(w):
        for a in range(16):
            tiles = [wt[pl.ds(16 * rev3(2 * w + k) + a, 8, stride=128), :] for k in range(2)]
            wtb16[pl.ds(64 * a + 16 * w, 16), :] = jnp.concatenate(tiles, axis=0).astype(BF16)

    loop(4, gather_a)

    def spread_a(s):
        rows = lax.broadcasted_iota(jnp.int32, (128, 256), 0)
        kind = lax.div(lax.broadcasted_iota(jnp.int32, (128, 256), 1), 128)
        chosen = (lax.rem(rows, 32) == 16 * kind + s) & (rows < 96)
        ones = jnp.where(chosen, 1.0, 0.0).astype(BF16)
        for half in range(4):
            r = jnp.dot(wtb16[256 * half : 256 * half + 256, :], ones, preferred_element_type=F32)
            wa[0, s, 4 * half : 4 * half + 4] = r[:, :128].reshape(4, 64, 128)
            wa[1, s, 4 * half : 4 * half + 4] = r[:, 128:].reshape(4, 64, 128)

    loop(7, spread_a)

    loads[2].wait()

    def convert(j):
        here = pl.ds(16 * j, 16)
        xs[here, :] = act[here, :].astype(F32)

    loop(64, convert)

    def forward_a(u):
        t = rev3(u)
        here = pl.ds(8 * u, 8)
        x = [xs[pl.ds(16 * t + a, 8, stride=128), :] for a in range(16)]
        for s in range(4):
            for a in range(16):
                fa[s, a, here, :] = x[a]
            x = forward_pairs(x, 2**s, lambda a: wa[0, s, a, here, :], lambda a: wa[1, s, a, here, :])
        for a in range(16):
            fa[4, a, here, :] = x[a]

    loop(8, forward_a)

    def tile(k):
        return slice(8 * k, 8 * k + 8)

    def finish_a(a):
        x = [fa[4, a, tile(u), :] for u in range(8)]
        for s in range(4, 7):
            if s > 4:
                for u in range(8):
                    fa[s, a, tile(u), :] = x[u]
            x = forward_pairs(
                x, 2 ** (6 - s), lambda u: wa[0, s, a, tile(u), :], lambda u: wa[1, s, a, tile(u), :]
            )
        for u in range(8):
            outa[a, tile(u), :] = x[u]

    loop(16, finish_a)

    pl.semaphore_wait(barrier, 30)

    def copy_w(g):
        return pltpu.make_async_remote_copy(
            src_ref=wmsg.at[rev4(g)], dst_ref=wbin.at[me], send_sem=s1.at[g], recv_sem=r1.at[me],
            device_id={"factor": g}, device_id_type=MESH,
        )

    def copy_x(g, w):
        return pltpu.make_async_remote_copy(
            src_ref=outa.at[rev4(g), pl.ds(8 * UP * w, 8 * UP)], dst_ref=inb.at[w, pl.ds(8 * UP * me, 8 * UP)],
            send_sem=s2.at[w, g], recv_sem=r2.at[w, me], device_id={"factor": g}, device_id_type=MESH,
        )

    def arrived(place, sem, axis, source):
        pltpu.make_async_remote_copy(
            src_ref=place, dst_ref=place, send_sem=sem, recv_sem=sem, device_id={axis: source}, device_id_type=MESH
        ).wait_recv()

    loop(15, lambda j: copy_x(peer(j, 1), 0).start())

    def pack_w(u):
        t = rev3(u)
        packed = [jnp.zeros((8, 128), F32) for kind in range(2)]
        for a in range(16):
            rows = wt[pl.ds(16 * t + a, 8, stride=128), :]
            for kind in range(2):
                moved = pltpu.roll(rows, (8 * a - 104 - 16 * kind) % 128, axis=1)
                packed[kind] = jnp.where(lax.div(lane, 8) == a, moved, packed[kind])
        for kind in range(2):
            wz[pl.ds(64 * kind + u, 8, stride=8), :] = packed[kind]

    loop(8, pack_w)
    wmsg[...] = wz[...].T.reshape(16, 8, 128)
    loop(15, lambda j: copy_w(peer(j, 1)).start())
    for w in range(1, PARTS):
        loop(15, lambda j: copy_x(peer(j, 1), w).start())
    wbin[me] = wmsg[mine]
    for w in range(PARTS):
        inb[w, pl.ds(8 * UP * me, 8 * UP), :] = outa[mine, 8 * UP * w : 8 * UP * w + 8 * UP, :]

    def column_ones(n):
        chosen = lax.rem(lax.broadcasted_iota(jnp.int32, (256, 128), 1), 8) == n
        ebc[n] = jnp.where(chosen, 1.0, 0.0).astype(BF16)

    loop(8, column_ones)

    loads[3].wait()

    def order_targets(u):
        for k in range(8):
            rows = tgt[pl.ds(128 * u + 16 * k, 16), :].astype(F32)
            p = rev_const(k, 3)
            ts[u, pl.ds(p, 8, stride=8), :] = rows[0:8]
            ts[u, pl.ds(64 + p, 8, stride=8), :] = rows[8:16]

    loop(8, order_targets)

    loop(15, lambda j: arrived(wbin.at[peer(j, -1)], r1.at[peer(j, -1)], "factor", peer(j, -1)))
    wflat = wbin[...].reshape(128, 128)
    wtb[0:128, :] = wflat
    wtb[128:256, :] = wflat.T

    def spread_b(u):
        for s in range(3):
            for h in range(2):
                rows = pltpu.roll(wtb[64 * h + s : 64 * h + s + 57 : 8, :], lax.rem(128 - u, 128), axis=1)
                for kind in range(2):
                    for p in range(8):
                        k = 64 * kind + 8 * p
                        w1[kind, s, u, 2 * p + h] = jnp.broadcast_to(rows[:, k : k + 1], (8, 128))
        for kind in range(2):
            rows = wtb[pl.ds(128 + 64 * kind + u, 8, stride=8), :]
            for s in range(4):
                for f in range(16):
                    k = 8 * f + 4 + s
                    w2[kind, s, u, f] = jnp.broadcast_to(rows[:, k : k + 1], (8, 128))

    def side_b(w, k):
        u = UP * w + k
        x = [inb[w, pl.ds(64 * UP * h + 8 * k + p, 8, stride=8 * UP), :] for p in range(8) for h in range(2)]
        for s in range(3):
            for i in range(16):
                f1[s, u, i] = x[i]
            x = forward_pairs(x, 2 ** (s + 1), lambda i: w1[0, s, u, i], lambda i: w1[1, s, u, i])
        for i in range(16):
            f2[0, u, pl.ds(64 * (i % 2) + i // 2, 8, stride=8), :] = x[i]
        x = [f2[0, u, tile(f), :] for f in range(16)]
        for s in range(4):
            if s > 0:
                for f in range(16):
                    f2[s, u, tile(f), :] = x[f]
            x = forward_pairs(x, 2**s, lambda f: w2[0, s, u, f], lambda f: w2[1, s, u, f])
        b = []
        for f in range(16):
            place = tile(rev_const(f, 4))
            error = x[f] - ts[u, place, :]
            es[u, place, :] = error
            b.append((2.0 / TOKENS) * error)
        for s in range(3, -1, -1):
            for f in range(16):
                b2[s, u, tile(f), :] = b[f]
            b = backward_pairs(b, 2**s, lambda f: w2[0, s, u, f], lambda f: w2[1, s, u, f])
        for f in range(16):
            b2[4, u, tile(f), :] = b[f]
        b = [b2[4, u, pl.ds(64 * h + p, 8, stride=8), :] for p in range(8) for h in range(2)]
        for s in range(2, -1, -1):
            for i in range(16):
                b1[s, u, i] = b[i]
            b = backward_pairs(b, 2 ** (s + 1), lambda i: w1[0, s, u, i], lambda i: w1[1, s, u, i])
        for i in range(16):
            outb[w, pl.ds(64 * UP * (i % 2) + 8 * k + i // 2, 8, stride=8 * UP), :] = b[i]

    def copy_b(f, w):
        return pltpu.make_async_remote_copy(
            src_ref=outb.at[w, pl.ds(8 * UP * f, 8 * UP)], dst_ref=ina.at[mine, pl.ds(8 * UP * w, 8 * UP)],
            send_sem=s3.at[w, f], recv_sem=r3.at[w, mine], device_id={"factor": f}, device_id_type=MESH,
        )

    def part_b(w):
        loop(UP, lambda k: spread_b(UP * w + k))
        loop(
            15,
            lambda j: arrived(
                inb.at[w, pl.ds(8 * UP * peer(14 - j, -1), 8 * UP)], r2.at[w, peer(14 - j, -1)], "factor", peer(14 - j, -1)
            ),
        )
        loop(UP, lambda k: side_b(w, k))
        loop(15, lambda j: copy_b(peer(j, 1), w).start())
        ina[mine, pl.ds(8 * UP * w, 8 * UP), :] = outb[w, pl.ds(8 * UP * me, 8 * UP), :]

    loop(PARTS, part_b)

    def order_errors(u):
        for k in range(8):
            p = rev_const(k, 3)
            for h in range(2):
                res[pl.ds(128 * u + 16 * k + 8 * h, 8), :] = es[u, pl.ds(64 * h + p, 8, stride=8), :]

    loop(8, order_errors)

    def grads_high(u):
        total = None
        for s in range(4):
            blocks = [
                b2[s, u, tile(f), :] * f2[s, u, tile(f ^ 2**s if kind else f), :] for kind in range(2) for f in range(16)
            ]
            term = lane_sums(blocks, 4 + s)
            total = term if total is None else total + term
        for kind in range(2):
            gz[pl.ds(64 * kind + u, 8, stride=8), :] = choose(tiles_of(total, kind))

    loop(8, grads_high)
    gt[...] = gz[...].T
    partb[...] = jnp.zeros_like(partb)

    def grads_low(u):
        for s in range(3):
            blocks = [
                b1[s, u, 2 * p + h] * f1[s, u, 2 * (p ^ 2**s if kind else p) + h]
                for h in range(2) for kind in range(2) for p in range(8)
            ]
            sums = lane_sums(blocks, u)
            for h in range(2):
                partb[s, h] = partb[s, h] + choose(tiles_of(sums, h))

    loop(8, grads_low)
    for s in range(3):
        for h in range(2):
            gt[64 * h + s : 64 * h + s + 57 : 8, :] = partb[s, h]

    def copy_g(f):
        return pltpu.make_async_remote_copy(
            src_ref=gt.at[pl.ds(8 * f, 8)], dst_ref=gin.at[pl.ds(8 * mine, 8)],
            send_sem=s4.at[f], recv_sem=r4.at[mine], device_id={"factor": f}, device_id_type=MESH,
        )

    loop(15, lambda j: copy_g(peer(j, 1)).start())
    gin[pl.ds(8 * mine, 8), :] = gt[pl.ds(8 * me, 8), :]

    def arrived_a(w):
        loop(
            15,
            lambda j: arrived(
                ina.at[rev4(peer(14 - j, -1)), pl.ds(8 * UP * w, 8 * UP)], r3.at[w, rev4(peer(14 - j, -1))],
                "factor", peer(14 - j, -1),
            ),
        )

    def level_a(s, u0):
        u1 = u0 + 2 ** (6 - s)
        rows = [pl.ds(8 * u0, 8), pl.ds(8 * u1, 8)]
        source = ina if s == 6 else b5.at[6 - s - 1]
        b = [[source[a, r, :] for r in rows] for a in range(16)]
        blocks = [
            b[a][k] * fa[s, a, rows[k ^ kind], :] for k in range(2) for kind in range(2) for a in range(16)
        ]
        sums = lane_sums(blocks, s)
        for k, u in ((0, u0), (1, u1)):
            for kind in range(2):
                term = choose(tiles_of(sums, 2 * k + kind))
                parta[kind, u] = term if s == 6 else parta[kind, u] + term
        for a in range(16):
            for k in range(2):
                b5[6 - s, a, rows[k], :] = (
                    wa[0, s, a, rows[k], :] * b[a][k] + wa[1, s, a, rows[1 - k], :] * b[a][1 - k]
                )

    for w in range(PARTS):
        arrived_a(w)
        if UP == 2:
            level_a(6, 2 * w)
            if w % 2 == 1:
                loop(2, lambda k: level_a(5, 2 * w - 2 + k))
        else:
            loop(UP // 2, lambda k: level_a(6, UP * w + 2 * k))
            loop(UP // 2, lambda k: level_a(5, UP * w + 4 * lax.div(k, 2) + lax.rem(k, 2)))
    loop(4, lambda k: level_a(4, k))

    def last_a(u):
        here = pl.ds(8 * u, 8)
        b = [b5[2, a, here, :] for a in range(16)]
        total = None
        for s in range(3, -1, -1):
            blocks = [b[a] * fa[s, a ^ (kind * 2**s), here, :] for kind in range(2) for a in range(16)]
            term = lane_sums(blocks, s)
            total = term if total is None else total + term
            if s > 0:
                b = backward_pairs(b, 2**s, lambda a: wa[0, s, a, here, :], lambda a: wa[1, s, a, here, :])
        for kind in range(2):
            gpart[pl.ds(128 * kind + u, 8, stride=16), :] = parta[kind, u] + choose(tiles_of(total, kind))

    loop(8, last_a)

    loop(15, lambda j: arrived(gin.at[pl.ds(8 * rev4(peer(j, -1)), 8)], r4.at[rev4(peer(j, -1))], "factor", peer(j, -1)))
    turned = gin[...].T
    for c in range(16):
        gpart[16 * c + 8 : 16 * c + 16, :] = turned[8 * c : 8 * c + 8]

    def copy_r(c):
        return pltpu.make_async_remote_copy(
            src_ref=gpart.at[pl.ds(16 * c, 16)], dst_ref=rs.at[col], send_sem=s5.at[c], recv_sem=r5.at[col],
            device_id={"col": c}, device_id_type=MESH,
        )

    def other(j):
        return lax.rem(col + 1 + j, 16)

    loop(15, lambda j: copy_r(other(j)).start())
    rs[col] = gpart[pl.ds(16 * col, 16), :]
    loop(15, lambda j: arrived(rs.at[other(j)], r5.at[other(j)], "col", other(j)))
    terms = [rs[c] for c in range(16)]
    while len(terms) > 1:
        terms = [terms[i] + terms[i + 1] for i in range(0, len(terms), 2)]
    gs[...] = terms[0]
    row_a = lax.rem(lax.broadcasted_iota(jnp.int32, (128, 128), 0), 16)
    lanes = lax.broadcasted_iota(jnp.int32, (128, 128), 1)
    out_row = lax.broadcasted_iota(jnp.int32, (16, 128), 0)
    out_lane = lax.broadcasted_iota(jnp.int32, (16, 128), 1)
    place = lax.rem(out_lane, 8)
    level_of = [place, 7 + place - jnp.where(place > 3, 1, 0)]
    valid = [place != 7, place != 3]
    own_a = lax.div(lanes, 8) == row_a
    total = jnp.zeros((16, 128), F32)
    for k in range(2):
        wide = jnp.concatenate(
            [jnp.broadcast_to(gs[8 * k + rev_const(t, 3) : 8 * k + rev_const(t, 3) + 1, :], (16, 128)) for t in range(8)], axis=0
        )
        wide = jnp.where(own_a, wide, 0.0)
        pick = jnp.where((level_of[k] == out_row) & valid[k], 1.0, 0.0).astype(BF16)
        for part in thirds(wide):
            total = total + lax.dot_general(
                pick, part.astype(BF16), (((1,), (1,)), ((), ())), preferred_element_type=F32
            )
    kind = lax.div(col, 8)
    here = pl.ds(pl.multiple_of(128 * lax.rem(col, 8), 128), 128)
    weights = jnp.where(kind == 0, dg[:, here], cr[:, here])
    gout[col, 0:14] = weights - step_scale * total[0:14]

    def copy_s(c):
        return pltpu.make_async_remote_copy(
            src_ref=gout.at[col], dst_ref=gout.at[col], send_sem=s6.at[c], recv_sem=r6.at[col],
            device_id={"col": c}, device_id_type=MESH,
        )

    loop(15, lambda j: copy_s(other(j)).start())
    loop(15, lambda j: arrived(gout.at[other(j)], r6.at[other(j)], "col", other(j)))
    for p in range(8):
        nd[:, 128 * p : 128 * p + 128] = gout[p, 0:14]
        nc[:, 128 * p : 128 * p + 128] = gout[8 + p, 0:14]

    def drain(j):
        g = peer(j, 1)
        copy_w(g).wait_send()
        copy_g(g).wait_send()
        for w in range(PARTS):
            copy_x(g, w).wait_send()
            copy_b(g, w).wait_send()
        copy_r(other(j)).wait_send()
        copy_s(other(j)).wait_send()

    loop(15, drain)


def write_out(a0, a1, a2, o0, o1, o2, sem):
    copies = [pltpu.make_async_copy(a, o, sem.at[k]) for k, (a, o) in enumerate([(a2, o2), (a0, o0), (a1, o1)])]
    for copy in copies:
        copy.start()
    for copy in copies:
        copy.wait()


def per_device(activations, targets, diagonal, crossing):
    height, width = activations.shape
    plain = lambda *shape: pltpu.VMEM(shape, F32)
    sems = lambda *shape: pltpu.SemaphoreType.DMA(shape)
    vmem, anywhere = pl.BlockSpec(memory_space=pltpu.VMEM), pl.BlockSpec(memory_space=pl.ANY)
    shapes = (diagonal.shape, crossing.shape, (height, width))
    results = pl.pallas_call(
        kernel,
        out_shape=tuple(pltpu.VMEM(shape, F32) for shape in shapes),
        in_specs=[anywhere] * 4,
        out_specs=(vmem,) * 3,
        scratch_shapes=[
            pltpu.VMEM((1024, 128), BF16), pltpu.VMEM((1024, 128), BF16),
            plain(14, 1024), plain(14, 1024),
            plain(1024, 128), plain(8, 128, 128), plain(8, 128, 128), plain(128, 1024), plain(1024, 128),
            pltpu.VMEM((1024, 128), BF16), pltpu.VMEM((8, 256, 128), BF16), plain(128, 128), plain(16, 8, 128), plain(16, 8, 128),
            plain(256, 128),
            plain(2, 7, 16, 64, 128), plain(2, 3, 8, 16, 8, 128), plain(2, 4, 8, 16, 8, 128),
            plain(7, 16, 64, 128), plain(3, 16, 64, 128),
            plain(3, 8, 16, 8, 128), plain(4, 8, 128, 128), plain(3, 8, 16, 8, 128), plain(5, 8, 128, 128),
            plain(16, 64, 128), plain(PARTS, 128 * UP, 128), plain(PARTS, 128 * UP, 128), plain(16, 64, 128),
            plain(2, 8, 8, 128), plain(3, 2, 8, 128), plain(128, 128), plain(128, 128), plain(128, 128),
            plain(256, 128), plain(16, 16, 128), plain(16, 128), plain(16, 16, 128),
            sems(4),
            sems(16), sems(16), sems(PARTS, 16), sems(PARTS, 16), sems(PARTS, 16), sems(PARTS, 16),
            sems(16), sems(16), sems(16), sems(16), sems(16), sems(16),
        ],
        compiler_params=pltpu.CompilerParams(
            collective_id=0, has_side_effects=True, vmem_limit_bytes=56 * 2**20
        ),
    )(activations, targets, diagonal, crossing)
    return pl.pallas_call(
        write_out,
        out_shape=tuple(jax.ShapeDtypeStruct(shape, F32) for shape in shapes),
        in_specs=[anywhere] * 3,
        out_specs=(anywhere,) * 3,
        scratch_shapes=[sems(3)],
        compiler_params=pltpu.CompilerParams(vmem_limit_bytes=2**20),
    )(*results)


def solution(mesh):
    placed = (P("factor", "col"), P("factor", "col"), P(None, "factor"), P(None, "factor"))
    return jax.shard_map(
        per_device,
        mesh=mesh,
        in_specs=placed,
        out_specs=(P(None, "factor"), P(None, "factor"), P("factor", "col")),
        check_vma=False,
    )
```

time: 425 us -> 59.1 us (0.14)
  waiting for transfers between devices: 272 us -> 0 us
  Pallas kernels: 0 us -> 58.4 us
  local copies, waits for them, and re-layouts: 46.9 us -> 0 us
  other arithmetic: 40.8 us -> 0 us
  starting transfers between devices: 28.5 us -> 0 us
  blocking collectives: 20 us -> 0 us
  between operations: 14.6 us -> 0.64 us
    ppermute x8 -> x0, waiting for transfers between devices: 135 us -> none  [partner(): return lax.ppermute(block, axis, route)]
    psum x1 -> x0, waiting for transfers between devices: 124 us -> none  [per_device(): grad_diag, grad_cross = lax.psum((grad_diag, grad_cross), 'col')]
    pallas_call x0 -> x2, Pallas kernels: none -> 58.4 us  [the longest x1 57.5 us: per_device(): pl.pallas_call(kernel, out_shape=tuple((pltpu.VMEM(shape, F32) for shape...]
    all_to_all x1 -> x0, blocking collectives: 20 us -> none  [per_device(): lax.all_to_all(to_owner(scaled, groups), 'factor', split_axis=1, concat_a...]
    ppermute x8 -> x0, starting transfers between devices: 19.8 us -> none  [partner(): return lax.ppermute(block, axis, route)]
    reduce_sum x13 -> x0, other arithmetic: 19.2 us -> none  [per_device(): cross_terms[level] = jnp.sum(gradient * beside, axis=1)]
    rev x19 -> x0, local copies, waits for them, and re-layouts: 17.5 us -> none  [partner_rows(): return jnp.flip(folded, 1).reshape(values.shape)]
    all_to_all x1 -> x0, waiting for transfers between devices: 13.3 us -> none  [per_device(): lax.all_to_all(to_owner(field, groups), 'factor', split_axis=1, concat_ax...]
  transfers between devices with their start and end apart: 10 -> 0, of which waited for: 10 -> 0; matrix products, arithmetic and copies ran while one was open for 0% -> 0% of each run, Pallas kernels for 0% -> 0%
where the time goes in v2:
time: 59.1 us; the launch traced here: 59 us
  Pallas kernels  58.4 us (99%)
  between operations  0.64 us (1%)
    pallas_call x1, Pallas kernels, per_device(): pl.pallas_call(kernel, out_shape=tuple((pltpu.VMEM(shape, F32) for shape...  57.5 us

profile of v2, /device:TPU:1, one launch (start us, length us, event | category | flops | bytes accessed | tf_op | source)
XLA Modules:
  0.0 59.0 jit_solution(9739095546018832521)
XLA Ops:
  0.6 57.5 %shard_map.67 = (f32[14,1024]{1,0:T(8,128)S(1)}, f32[14,1024]{1,0:T(8,128)S(1)}, f32[1024,128]{1,0:T(8,128)S(1)}) custom-call(bf16[1024,128]{1,0:T(8,128)(2,1)} %act_hbm.1, bf16[1024,128]{1,0:T(8,128)(2,1)} %tgt_hbm.1, f32[14,1024]{1,0:T(8,128)} %dg_hbm.1, f32[14,1024]{1,0:T(8,128)} %cr_hbm.1), custom_call_target="tpu_custom_call" | custom-call | tf_op jit(solution)/shard_map/pallas_call | solution.py:506
  58.2 0.9 %shard_map.68 = (f32[14,1024]{1,0:T(8,128)}, f32[14,1024]{1,0:T(8,128)}, f32[1024,128]{1,0:T(8,128)}) custom-call(f32[14,1024]{1,0:T(8,128)S(1)} %get-tuple-element.6.a0, f32[14,1024]{1,0:T(8,128)S(1)} %get-tuple-element.7.a1, f32[1024,128]{1,0:T(8,128)S(1)} %get-tuple-element.8.a2), custom_call_target="tpu_custom_call" | custom-call | tf_op jit(solution)/shard_map/pallas_call | solution.py:531

commit v3 on v2

--- a/solution.py
+++ b/solution.py
@@ -42,12 +42,12 @@
     return [diag(i) * b[i] + carried[i ^ span] for i in range(len(b))]
 
 
-def loop(count, body):
+def loop(count, body, unroll=1):
     def step(j, carry):
         body(j)
         return carry
 
-    lax.fori_loop(0, count, step, 0)
+    lax.fori_loop(0, count, step, 0, unroll=unroll)
 
 
 def thirds(value):
@@ -61,7 +61,7 @@
     act_hbm, tgt_hbm, dg_hbm, cr_hbm,
     nd, nc, res,
     act, tgt, dg, cr,
-    xs, ts, es, wst, wt, wtb16, ebc, wz, wmsg, wbin, wtb,
+    xs, ts, es, wst, wt, ewc, ebc, wz, wmsg, wbin, wtb,
     wa, w1, w2, fa, b5, f1, f2, b1, b2,
     outa, inb, outb, ina, parta, partb, gz, gt, gin, gpart, rs, gs, gout,
     ld, s1, r1, s2, r2, s3, r3, s4, r4, s5, r5, s6, r6,
@@ -73,27 +73,25 @@
 
     loads = [
         pltpu.make_async_copy(a, b, ld.at[k])
-        for k, (a, b) in enumerate([(dg_hbm, dg), (cr_hbm, cr), (act_hbm, act), (tgt_hbm, tgt)])
+        for k, (a, b) in enumerate([(act_hbm, act), (dg_hbm, dg), (cr_hbm, cr), (tgt_hbm, tgt)])
     ]
     for copy in loads:
         copy.start()
 
     barrier = pltpu.get_barrier_semaphore()
-
-    def greet(j):
-        pl.semaphore_signal(
-            barrier, inc=1, device_id={"factor": lax.rem(me + 1 + j, 16)}, device_id_type=MESH
-        )
-        pl.semaphore_signal(
-            barrier, inc=1, device_id={"col": lax.rem(col + 1 + j, 16)}, device_id_type=MESH
-        )
-
-    loop(15, greet)
 
     def peer(j, sign):
         dx = 1 - lax.div(j, 8)
         dz = lax.rem(dx * (j + 4) + (1 - dx) * (j - 7), 8)
         return lax.rem(mx + dx, 2) * 8 + lax.rem(mz + sign * dz + 8, 8)
+
+    def greet(j):
+        pl.semaphore_signal(barrier, inc=1, device_id={"factor": peer(j, 1)}, device_id_type=MESH)
+        pl.semaphore_signal(
+            barrier, inc=1, device_id={"col": lax.rem(col + 1 + j, 16)}, device_id_type=MESH
+        )
+
+    loop(15, greet)
 
     lane = lax.broadcasted_iota(jnp.int32, (8, 128), 1)
     lane_low = [lax.rem(lax.div(lane, 2**k), 2) == 0 for k in range(7)]
@@ -114,9 +112,24 @@
     def tiles_of(block, k):
         return [block[128 * k + 8 * i : 128 * k + 8 * i + 8] for i in range(16)]
 
+    def column_pairs(s):
+        rows = lax.broadcasted_iota(jnp.int32, (128, 256), 0)
+        kind = lax.div(lax.broadcasted_iota(jnp.int32, (128, 256), 1), 128)
+        chosen = (lax.rem(rows, 32) == 16 * kind + s) & (rows < 96)
+        ewc[s] = jnp.where(chosen, 1.0, 0.0).astype(BF16)
+
+    loop(7, column_pairs)
+
     wst[96:128, :] = jnp.zeros((32, 1024), F32)
     loads[0].wait()
+
+    def convert(j):
+        here = pl.ds(16 * j, 16)
+        xs[here, :] = act[here, :].astype(F32)
+
+    loop(64, convert, 4)
     loads[1].wait()
+    loads[2].wait()
     for s in range(14):
         row = 96 + (s if s < 7 else 8 + slot(s - 7))
         wst[row : row + 1, :] = dg[s : s + 1, :]
@@ -128,45 +141,27 @@
     for k in range(8):
         wt[128 * k : 128 * k + 128, :] = wst[:, 128 * k : 128 * k + 128].T
 
-    def gather_a(w):
-        for a in range(16):
-            tiles = [wt[pl.ds(16 * rev3(2 * w + k) + a, 8, stride=128), :] for k in range(2)]
-            wtb16[pl.ds(64 * a + 16 * w, 16), :] = jnp.concatenate(tiles, axis=0).astype(BF16)
-
-    loop(4, gather_a)
-
-    def spread_a(s):
-        rows = lax.broadcasted_iota(jnp.int32, (128, 256), 0)
-        kind = lax.div(lax.broadcasted_iota(jnp.int32, (128, 256), 1), 128)
-        chosen = (lax.rem(rows, 32) == 16 * kind + s) & (rows < 96)
-        ones = jnp.where(chosen, 1.0, 0.0).astype(BF16)
-        for half in range(4):
-            r = jnp.dot(wtb16[256 * half : 256 * half + 256, :], ones, preferred_element_type=F32)
-            wa[0, s, 4 * half : 4 * half + 4] = r[:, :128].reshape(4, 64, 128)
-            wa[1, s, 4 * half : 4 * half + 4] = r[:, 128:].reshape(4, 64, 128)
-
-    loop(7, spread_a)
-
-    loads[2].wait()
-
-    def convert(j):
-        here = pl.ds(16 * j, 16)
-        xs[here, :] = act[here, :].astype(F32)
-
-    loop(64, convert)
-
     def forward_a(u):
         t = rev3(u)
         here = pl.ds(8 * u, 8)
+        rows = [wt[pl.ds(16 * t + a, 8, stride=128), :] for a in range(16)]
+        columns = jnp.concatenate(rows, axis=0).astype(BF16)
         x = [xs[pl.ds(16 * t + a, 8, stride=128), :] for a in range(16)]
-        for s in range(4):
+        for s in range(7):
+            wide = jnp.dot(columns, ewc[s], preferred_element_type=F32)
+            own = [wide[8 * a : 8 * a + 8, 0:128] for a in range(16)]
+            beside = [wide[8 * a : 8 * a + 8, 128:256] for a in range(16)]
             for a in range(16):
-                fa[s, a, here, :] = x[a]
-            x = forward_pairs(x, 2**s, lambda a: wa[0, s, a, here, :], lambda a: wa[1, s, a, here, :])
+                wa[0, s, a, here, :] = own[a]
+                wa[1, s, a, here, :] = beside[a]
+            if s < 4:
+                for a in range(16):
+                    fa[s, a, here, :] = x[a]
+                x = forward_pairs(x, 2**s, lambda a: own[a], lambda a: beside[a])
         for a in range(16):
             fa[4, a, here, :] = x[a]
 
-    loop(8, forward_a)
+    loop(8, forward_a, 4)
 
     def tile(k):
         return slice(8 * k, 8 * k + 8)
@@ -183,7 +178,7 @@
         for u in range(8):
             outa[a, tile(u), :] = x[u]
 
-    loop(16, finish_a)
+    loop(16, finish_a, 4)
 
     pl.semaphore_wait(barrier, 30)
 
@@ -217,7 +212,7 @@
         for kind in range(2):
             wz[pl.ds(64 * kind + u, 8, stride=8), :] = packed[kind]
 
-    loop(8, pack_w)
+    loop(8, pack_w, 2)
     wmsg[...] = wz[...].T.reshape(16, 8, 128)
     loop(15, lambda j: copy_w(peer(j, 1)).start())
     for w in range(1, PARTS):
@@ -305,14 +300,14 @@
         )
 
     def part_b(w):
-        loop(UP, lambda k: spread_b(UP * w + k))
+        loop(UP, lambda k: spread_b(UP * w + k), 2)
         loop(
             15,
             lambda j: arrived(
                 inb.at[w, pl.ds(8 * UP * peer(14 - j, -1), 8 * UP)], r2.at[w, peer(14 - j, -1)], "factor", peer(14 - j, -1)
             ),
         )
-        loop(UP, lambda k: side_b(w, k))
+        loop(UP, lambda k: side_b(w, k), 2)
         loop(15, lambda j: copy_b(peer(j, 1), w).start())
         ina[mine, pl.ds(8 * UP * w, 8 * UP), :] = outb[w, pl.ds(8 * UP * me, 8 * UP), :]
 
@@ -364,6 +359,14 @@
 
     loop(15, lambda j: copy_g(peer(j, 1)).start())
     gin[pl.ds(8 * mine, 8), :] = gt[pl.ds(8 * me, 8), :]
+
+    def drain_first(j):
+        g = peer(j, 1)
+        copy_w(g).wait_send()
+        for w in range(PARTS):
+            copy_x(g, w).wait_send()
+
+    loop(15, drain_first)
 
     def arrived_a(w):
         loop(
@@ -398,11 +401,11 @@
         if UP == 2:
             level_a(6, 2 * w)
             if w % 2 == 1:
-                loop(2, lambda k: level_a(5, 2 * w - 2 + k))
+                loop(2, lambda k: level_a(5, 2 * w - 2 + k), 2)
         else:
             loop(UP // 2, lambda k: level_a(6, UP * w + 2 * k))
             loop(UP // 2, lambda k: level_a(5, UP * w + 4 * lax.div(k, 2) + lax.rem(k, 2)))
-    loop(4, lambda k: level_a(4, k))
+    loop(4, lambda k: level_a(4, k), 2)
 
     def last_a(u):
         here = pl.ds(8 * u, 8)
@@ -417,7 +420,7 @@
         for kind in range(2):
             gpart[pl.ds(128 * kind + u, 8, stride=16), :] = parta[kind, u] + choose(tiles_of(total, kind))
 
-    loop(8, last_a)
+    loop(8, last_a, 4)
 
     loop(15, lambda j: arrived(gin.at[pl.ds(8 * rev4(peer(j, -1)), 8)], r4.at[rev4(peer(j, -1))], "factor", peer(j, -1)))
     turned = gin[...].T
@@ -435,6 +438,13 @@
 
     loop(15, lambda j: copy_r(other(j)).start())
     rs[col] = gpart[pl.ds(16 * col, 16), :]
+    def drain_second(j):
+        g = peer(j, 1)
+        copy_g(g).wait_send()
+        for w in range(PARTS):
+            copy_b(g, w).wait_send()
+
+    loop(15, drain_second)
     loop(15, lambda j: arrived(rs.at[other(j)], r5.at[other(j)], "col", other(j)))
     terms = [rs[c] for c in range(16)]
     while len(terms) > 1:
@@ -471,22 +481,13 @@
         )
 
     loop(15, lambda j: copy_s(other(j)).start())
+    loop(15, lambda j: copy_r(other(j)).wait_send())
     loop(15, lambda j: arrived(gout.at[other(j)], r6.at[other(j)], "col", other(j)))
     for p in range(8):
         nd[:, 128 * p : 128 * p + 128] = gout[p, 0:14]
         nc[:, 128 * p : 128 * p + 128] = gout[8 + p, 0:14]
 
-    def drain(j):
-        g = peer(j, 1)
-        copy_w(g).wait_send()
-        copy_g(g).wait_send()
-        for w in range(PARTS):
-            copy_x(g, w).wait_send()
-            copy_b(g, w).wait_send()
-        copy_r(other(j)).wait_send()
-        copy_s(other(j)).wait_send()
-
-    loop(15, drain)
+    loop(15, lambda j: copy_s(other(j)).wait_send())
 
 
 def write_out(a0, a1, a2, o0, o1, o2, sem):
@@ -512,7 +513,7 @@
             pltpu.VMEM((1024, 128), BF16), pltpu.VMEM((1024, 128), BF16),
             plain(14, 1024), plain(14, 1024),
             plain(1024, 128), plain(8, 128, 128), plain(8, 128, 128), plain(128, 1024), plain(1024, 128),
-            pltpu.VMEM((1024, 128), BF16), pltpu.VMEM((8, 256, 128), BF16), plain(128, 128), plain(16, 8, 128), plain(16, 8, 128),
+            pltpu.VMEM((7, 128, 256), BF16), pltpu.VMEM((8, 256, 128), BF16), plain(128, 128), plain(16, 8, 128), plain(16, 8, 128),
             plain(256, 128),
             plain(2, 7, 16, 64, 128), plain(2, 3, 8, 16, 8, 128), plain(2, 4, 8, 16, 8, 128),
             plain(7, 16, 64, 128), plain(3, 16, 64, 128),

time: 59.1 us -> 55.7 us (0.942)
  Pallas kernels: 58.4 us -> 55 us
    pallas_call x1, Pallas kernels: 57.5 us -> 54.1 us  [per_device(): pl.pallas_call(kernel, out_shape=tuple((pltpu.VMEM(shape, F32) for shape...]
where the time goes in v3:
time: 55.7 us; the launch traced here: 55.6 us
  Pallas kernels  55 us (99%)
  between operations  0.64 us (1%)
    pallas_call x1, Pallas kernels, per_device(): pl.pallas_call(kernel, out_shape=tuple((pltpu.VMEM(shape, F32) for shape...  54.1 us

profile of v3, /device:TPU:1, one launch (start us, length us, event | category | flops | bytes accessed | tf_op | source)
XLA Modules:
  0.0 55.6 jit_solution(17250646279476688095)
XLA Ops:
  0.6 54.1 %shard_map.67 = (f32[14,1024]{1,0:T(8,128)S(1)}, f32[14,1024]{1,0:T(8,128)S(1)}, f32[1024,128]{1,0:T(8,128)S(1)}) custom-call(bf16[1024,128]{1,0:T(8,128)(2,1)} %act_hbm.1, bf16[1024,128]{1,0:T(8,128)(2,1)} %tgt_hbm.1, f32[14,1024]{1,0:T(8,128)} %dg_hbm.1, f32[14,1024]{1,0:T(8,128)} %cr_hbm.1), custom_call_target="tpu_custom_call" | custom-call | tf_op jit(solution)/shard_map/pallas_call | solution.py:507
  54.8 0.9 %shard_map.68 = (f32[14,1024]{1,0:T(8,128)}, f32[14,1024]{1,0:T(8,128)}, f32[1024,128]{1,0:T(8,128)}) custom-call(f32[14,1024]{1,0:T(8,128)S(1)} %get-tuple-element.6.a0, f32[14,1024]{1,0:T(8,128)S(1)} %get-tuple-element.7.a1, f32[1024,128]{1,0:T(8,128)S(1)} %get-tuple-element.8.a2), custom_call_target="tpu_custom_call" | custom-call | tf_op jit(solution)/shard_map/pallas_call | solution.py:532

commit v4 on v3

--- a/solution.py
+++ b/solution.py
@@ -161,7 +161,7 @@
         for a in range(16):
             fa[4, a, here, :] = x[a]
 
-    loop(8, forward_a, 4)
+    loop(8, forward_a, 8)
 
     def tile(k):
         return slice(8 * k, 8 * k + 8)
@@ -178,7 +178,7 @@
         for u in range(8):
             outa[a, tile(u), :] = x[u]
 
-    loop(16, finish_a, 4)
+    loop(16, finish_a, 8)
 
     pl.semaphore_wait(barrier, 30)
 
@@ -212,7 +212,7 @@
         for kind in range(2):
             wz[pl.ds(64 * kind + u, 8, stride=8), :] = packed[kind]
 
-    loop(8, pack_w, 2)
+    loop(8, pack_w, 4)
     wmsg[...] = wz[...].T.reshape(16, 8, 128)
     loop(15, lambda j: copy_w(peer(j, 1)).start())
     for w in range(1, PARTS):
@@ -405,7 +405,7 @@
         else:
             loop(UP // 2, lambda k: level_a(6, UP * w + 2 * k))
             loop(UP // 2, lambda k: level_a(5, UP * w + 4 * lax.div(k, 2) + lax.rem(k, 2)))
-    loop(4, lambda k: level_a(4, k), 2)
+    loop(4, lambda k: level_a(4, k), 4)
 
     def last_a(u):
         here = pl.ds(8 * u, 8)
@@ -420,7 +420,7 @@
         for kind in range(2):
             gpart[pl.ds(128 * kind + u, 8, stride=16), :] = parta[kind, u] + choose(tiles_of(total, kind))
 
-    loop(8, last_a, 4)
+    loop(8, last_a, 8)
 
     loop(15, lambda j: arrived(gin.at[pl.ds(8 * rev4(peer(j, -1)), 8)], r4.at[rev4(peer(j, -1))], "factor", peer(j, -1)))
     turned = gin[...].T

time: 55.7 us -> 54.9 us (0.986)
  Pallas kernels: 55 us -> 54.2 us
    pallas_call x1, Pallas kernels: 54.1 us -> 53.3 us  [per_device(): pl.pallas_call(kernel, out_shape=tuple((pltpu.VMEM(shape, F32) for shape...]
where the time goes in v4:
time: 54.9 us; the launch traced here: 54.8 us
  Pallas kernels  54.2 us (99%)
  between operations  0.64 us (1%)
    pallas_call x1, Pallas kernels, per_device(): pl.pallas_call(kernel, out_shape=tuple((pltpu.VMEM(shape, F32) for shape...  53.3 us

profile of v4, /device:TPU:1, one launch (start us, length us, event | category | flops | bytes accessed | tf_op | source)
XLA Modules:
  0.0 54.8 jit_solution(9081341241102512149)
XLA Ops:
  0.6 53.3 %shard_map.67 = (f32[14,1024]{1,0:T(8,128)S(1)}, f32[14,1024]{1,0:T(8,128)S(1)}, f32[1024,128]{1,0:T(8,128)S(1)}) custom-call(bf16[1024,128]{1,0:T(8,128)(2,1)} %act_hbm.1, bf16[1024,128]{1,0:T(8,128)(2,1)} %tgt_hbm.1, f32[14,1024]{1,0:T(8,128)} %dg_hbm.1, f32[14,1024]{1,0:T(8,128)} %cr_hbm.1), custom_call_target="tpu_custom_call" | custom-call | tf_op jit(solution)/shard_map/pallas_call | solution.py:507
  54.0 0.9 %shard_map.68 = (f32[14,1024]{1,0:T(8,128)}, f32[14,1024]{1,0:T(8,128)}, f32[1024,128]{1,0:T(8,128)}) custom-call(f32[14,1024]{1,0:T(8,128)S(1)} %get-tuple-element.6.a0, f32[14,1024]{1,0:T(8,128)S(1)} %get-tuple-element.7.a1, f32[1024,128]{1,0:T(8,128)S(1)} %get-tuple-element.8.a2), custom_call_target="tpu_custom_call" | custom-call | tf_op jit(solution)/shard_map/pallas_call | solution.py:532

commit v5 on v4

--- a/solution.py
+++ b/solution.py
@@ -180,27 +180,6 @@
 
     loop(16, finish_a, 8)
 
-    pl.semaphore_wait(barrier, 30)
-
-    def copy_w(g):
-        return pltpu.make_async_remote_copy(
-            src_ref=wmsg.at[rev4(g)], dst_ref=wbin.at[me], send_sem=s1.at[g], recv_sem=r1.at[me],
-            device_id={"factor": g}, device_id_type=MESH,
-        )
-
-    def copy_x(g, w):
-        return pltpu.make_async_remote_copy(
-            src_ref=outa.at[rev4(g), pl.ds(8 * UP * w, 8 * UP)], dst_ref=inb.at[w, pl.ds(8 * UP * me, 8 * UP)],
-            send_sem=s2.at[w, g], recv_sem=r2.at[w, me], device_id={"factor": g}, device_id_type=MESH,
-        )
-
-    def arrived(place, sem, axis, source):
-        pltpu.make_async_remote_copy(
-            src_ref=place, dst_ref=place, send_sem=sem, recv_sem=sem, device_id={axis: source}, device_id_type=MESH
-        ).wait_recv()
-
-    loop(15, lambda j: copy_x(peer(j, 1), 0).start())
-
     def pack_w(u):
         t = rev3(u)
         packed = [jnp.zeros((8, 128), F32) for kind in range(2)]
@@ -214,6 +193,27 @@
 
     loop(8, pack_w, 4)
     wmsg[...] = wz[...].T.reshape(16, 8, 128)
+    pl.semaphore_wait(barrier, 30)
+
+    def copy_w(g):
+        return pltpu.make_async_remote_copy(
+            src_ref=wmsg.at[rev4(g)], dst_ref=wbin.at[me], send_sem=s1.at[g], recv_sem=r1.at[me],
+            device_id={"factor": g}, device_id_type=MESH,
+        )
+
+    def copy_x(g, w):
+        return pltpu.make_async_remote_copy(
+            src_ref=outa.at[rev4(g), pl.ds(8 * UP * w, 8 * UP)], dst_ref=inb.at[w, pl.ds(8 * UP * me, 8 * UP)],
+            send_sem=s2.at[w, g], recv_sem=r2.at[w, me], device_id={"factor": g}, device_id_type=MESH,
+        )
+
+    def arrived(place, sem, axis, source):
+        pltpu.make_async_remote_copy(
+            src_ref=place, dst_ref=place, send_sem=sem, recv_sem=sem, device_id={axis: source}, device_id_type=MESH
+        ).wait_recv()
+
+    loop(15, lambda j: copy_x(peer(j, 1), 0).start())
+
     loop(15, lambda j: copy_w(peer(j, 1)).start())
     for w in range(1, PARTS):
         loop(15, lambda j: copy_x(peer(j, 1), w).start())

time: 54.9 us -> 55.6 us (1.013)
  Pallas kernels: 54.2 us -> 54.8 us
    pallas_call x1, Pallas kernels: 53.3 us -> 54 us  [per_device(): pl.pallas_call(kernel, out_shape=tuple((pltpu.VMEM(shape, F32) for shape...]
where the time goes in v5:
time: 55.6 us; the launch traced here: 55.5 us
  Pallas kernels  54.8 us (99%)
  between operations  0.64 us (1%)
    pallas_call x1, Pallas kernels, per_device(): pl.pallas_call(kernel, out_shape=tuple((pltpu.VMEM(shape, F32) for shape...  54 us

profile of v5, /device:TPU:1, one launch (start us, length us, event | category | flops | bytes accessed | tf_op | source)
XLA Modules:
  0.0 55.5 jit_solution(12290078991623404728)
XLA Ops:
  0.6 54.0 %shard_map.67 = (f32[14,1024]{1,0:T(8,128)S(1)}, f32[14,1024]{1,0:T(8,128)S(1)}, f32[1024,128]{1,0:T(8,128)S(1)}) custom-call(bf16[1024,128]{1,0:T(8,128)(2,1)} %act_hbm.1, bf16[1024,128]{1,0:T(8,128)(2,1)} %tgt_hbm.1, f32[14,1024]{1,0:T(8,128)} %dg_hbm.1, f32[14,1024]{1,0:T(8,128)} %cr_hbm.1), custom_call_target="tpu_custom_call" | custom-call | tf_op jit(solution)/shard_map/pallas_call | solution.py:507
  54.6 0.9 %shard_map.68 = (f32[14,1024]{1,0:T(8,128)}, f32[14,1024]{1,0:T(8,128)}, f32[1024,128]{1,0:T(8,128)}) custom-call(f32[14,1024]{1,0:T(8,128)S(1)} %get-tuple-element.6.a0, f32[14,1024]{1,0:T(8,128)S(1)} %get-tuple-element.7.a1, f32[1024,128]{1,0:T(8,128)S(1)} %get-tuple-element.8.a2), custom_call_target="tpu_custom_call" | custom-call | tf_op jit(solution)/shard_map/pallas_call | solution.py:532
